TPU v7x, 256 devices: a whole 4x4x8 slice. The times are simulated.
256 devices in a mesh: ma: 64 (over z, x, core), row: 4 (over y).
Axes of the slice: x: 4, y: 4, z: 8, core: 2. Of those that a mesh axis runs over, the one named last changes fastest.
Arguments:
- nonlinear: bfloat16 [128, 1536, 4, 512], P('ma', None, None, 'row'), may hold values from -6 to 6
- legendre: bfloat16 [128, 768, 2, 512], P('ma'), may hold values from -0.15625 to 0.15625
- inverse: bfloat16 [2, 512, 2, 512, 512], P(None, 'ma', None, 'row'), may hold values from -0.25 to 0.25
- orders: int32 [128], P('ma'), may hold values from 0 to 1023, as said below
Outputs:
- solved: bfloat16 [128, 2, 512, 4, 512], P('ma', None, None, None, 'row')
Inputs may be any that keep to these rules, and one draw needn't show every extreme that they name: The orders are distinct; slots 2 i and 2 i + 1 hold m and 1023 - m with m < 512, so every index of ma holds whole pairs.
All inputs are finite; a program needn't handle non-finite values.
Results may differ from a plain program's by a relative error of at most 0.0059.
Values may be sent and summed in bfloat16 or wider, within the bound.
A program may use at most 128 MiB of HBM per device.

v0:
```python
import jax
import jax.numpy as jnp
from jax import lax
from jax.sharding import PartitionSpec as P


def radial_step(coeff_block, inverse_part):
    arrived = lax.all_to_all(coeff_block, "ma", split_axis=2, concat_axis=0, tiled=True)
    order_total, parity_count, degree_block, part_count, radial_rows = arrived.shape
    field_count = inverse_part.shape[2]
    separated = arrived.reshape(
        order_total, parity_count, degree_block, field_count, 2, radial_rows
    )
    summed = jnp.einsum(
        "pjfrs,mpjfks->mpjfkr",
        inverse_part,
        lax.all_gather(separated, "row", axis=5, tiled=True),
        preferred_element_type=jnp.float32,
    )
    returned = summed.astype(jnp.bfloat16).reshape(
        order_total, parity_count, degree_block, part_count, radial_rows
    )
    return lax.all_to_all(returned, "ma", split_axis=0, concat_axis=2, tiled=True)


def per_device(nonlinear, legendre, inverse, orders):
    order_count, theta_count, part_count, radial_rows = nonlinear.shape
    half_theta = theta_count // 2
    half_degree = legendre.shape[3]
    flattened = nonlinear.reshape(order_count, theta_count, part_count * radial_rows)
    northern = flattened[:, :half_theta].astype(jnp.float32)
    southern = flattened[:, half_theta:][:, ::-1].astype(jnp.float32)
    even_part = (northern + southern).astype(jnp.bfloat16)
    odd_part = (northern - southern).astype(jnp.bfloat16)
    degree_half = lax.iota(jnp.int32, half_degree)

    def analyse(parity):
        chosen = jnp.where(((orders + parity) % 2 == 0)[:, None, None], even_part, odd_part)
        table_part = legendre[:, :, parity, :]
        product = jnp.einsum("mhj,mhx->mjx", table_part, chosen, preferred_element_type=jnp.float32)
        live_mask = 2 * degree_half[None, :] + parity >= orders[:, None]
        product = jnp.where(live_mask[:, :, None], product, 0.0)
        return product.astype(jnp.bfloat16).reshape(
            order_count, 1, half_degree, part_count, radial_rows
        )

    coefficients = jnp.concatenate([analyse(0), analyse(1)], axis=1)
    return radial_step(coefficients, inverse)


def solution(mesh):
    in_specs = (
        P("ma", None, None, "row"),
        P("ma", None, None, None),
        P(None, "ma", None, "row", None),
        P("ma"),
    )
    out_specs = P("ma", None, None, None, "row")
    return jax.shard_map(
        per_device, mesh=mesh, in_specs=in_specs, out_specs=out_specs, check_vma=False
    )
```

profile of v0, /device:TPU:1, one launch (start us, length us, event | category | flops | bytes accessed | tf_op | source)
XLA Modules:
  0.0 288.7 jit_solution(4184743862048138473)
XLA Ops:
  6.5 0.0 all-gather.2.cloned.1.call-start
  6.5 0.7 fusion.15
  7.2 4.3 %copy.30 = bf16[2,1536,4,128]{1,3,2,0:T(8,128)(2,1)S(1)} copy(bf16[2,1536,4,128]{3,2,1,0:T(4,128)(2,1)} %param.4) | data formatting | bytes 6291456 | tf_op jit(solution)/shard_map/reshape | solution.py:30
  11.5 0.0 copy-start.1
  11.6 1.7 copy-done.1
  13.2 1.2 slice.17
  14.5 0.0 copy-start
  14.5 24.4 %rev.3 = bf16[2,768,512]{1,2,0:T(8,128)(2,1)} reverse(bf16[2,768,512]{1,2,0:T(8,128)(2,1)} %slice.17), dimensions={1} | reverse | bytes 3145728 | tf_op jit(solution)/shard_map/rev | solution.py:32
  38.8 0.0 copy-done
  38.8 0.0 copy-start.6
  38.8 0.0 copy-start.2
  38.8 0.0 copy-start.5
  38.9 5.4 %fusion.19 = (bf16[2,768,1,512]{3,2,1,0:T(2,128)(2,1)}, bf16[2,768,1,512]{3,2,1,0:T(2,128)(2,1)S(1)}) fusion(bf16[2,768,2,512]{3,2,1,0:T(2,128)(2,1)S(1)} %copy-done), kind=kLoop, calls=%fused_computation.31 | loop fusion | bytes 6291456 | tf_op jit(solution)/shard_map/slice | solution.py:39
  44.2 0.0 copy-done.6
  44.2 0.1 broadcast_compare_fusion.1
  44.3 0.0 copy-done.2
  44.3 0.0 copy-done.5
  44.3 0.0 copy-start.3
  44.3 2.0 select_convert_fusion
  46.3 2.5 copy.24
  48.8 0.0 copy-done.3
  48.8 4.4 %select_convert_fusion.1 = bf16[2,512,512]{2,1,0:T(8,128)(2,1)} fusion(bf16[2,768,1,512]{3,2,1,0:T(2,128)(2,1)} %get-tuple-element.5, pred[2]{0:T(512)(128)(4,1)S(1)} %get-tuple-element.9, pred[2,512]{1,0:T(4,128)(4,1)S(1)} %get-tuple-element.7, bf16[2,768,512]{1,2,0:T(8,128)(2,1)} %rev.3, bf16[2,1536,512]{1,2,0:T(8,128)(2,1)S(1)} %bitcast.39), kind=kOutput, calls=%fused_computation.9 | convolution fusion | flops 811859968 | bytes 5769728 | tf_op jit(solution)/shard_map/mhj,mhx->mjx/dot_general | solution.py:40
  53.2 0.0 copy-start.4
  53.2 1.8 copy.23
  55.0 0.0 copy-done.4
  55.0 1.5 pad_maximum_fusion
  56.5 62.5 %all_to_all.33 = bf16[2,2,512,4,128]{4,3,1,0,2:T(4,128)(2,1)S(1)} all-to-all(bf16[2,2,512,4,128]{4,3,1,0,2:T(4,128)(2,1)S(1)} %pad_maximum_fusion), channel_id=1, replica_groups=mesh['ma'=64,'row'=4] {'ma'}, dimensions={2} | all-to-all | bytes 4194304 | tf_op jit(solution)/shard_map/all_to_all | solution.py:8
  119.0 0.5 copy.38
  119.5 3.5 %copy.26 = bf16[64,2,2,8,4,128]{5,1,0,4,3,2:T(2,128)(2,1)} copy(bf16[64,2,2,8,4,128]{5,3,0,4,2,1:T(8,128)(2,1)S(1)} %bitcast.35) | data formatting | bytes 4194304 | tf_op jit(solution)/shard_map/all_to_all | solution.py:8
  123.0 0.0 all-gather.2.cloned.1.call-update
  123.0 86.8 %all-gather.2.cloned.1.call-done = bf16[128,2,8,2,2,512]{5,0,4,3,2,1:T(8,128)(2,1)} async-done(((bf16[128,2,8,2,2,128]{5,0,4,3,2,1:T(8,128)(2,1)}), bf16[128,2,8,2,2,512]{5,0,4,3,2,1:T(8,128)(2,1)}) %all-gather.2.cloned.1.call-update) | async-done | bytes 8388624 | tf_op jit(solution)/shard_map/all_gather | solution.py:17
  209.8 6.9 %fusion.4 = bf16[2,8,2,128,2,128]{5,3,4,2,1,0:T(8,128)(2,1)S(1)} fusion(bf16[128,2,8,2,2,512]{5,0,4,3,2,1:T(8,128)(2,1)} %all-gather.2.cloned.1.call-done, bf16[2,8,2,128,512]{4,3,2,1,0:T(8,128)(2,1)} %param.6), kind=kOutput, calls=%fused_computation.10 | convolution fusion | flops 1074790400 | bytes 14680064 | tf_op jit(solution)/shard_map/pjfrs,mpjfks->mpjfkr/dot_general | solution.py:14
  216.7 1.6 copy.27
  218.3 61.4 %all_to_all.34 = bf16[128,2,8,4,128]{4,3,2,1,0:T(4,128)(2,1)S(1)} all-to-all(bf16[128,2,8,4,128]{4,3,2,1,0:T(4,128)(2,1)S(1)} %copy.27), channel_id=1, replica_groups=mesh['ma'=64,'row'=4] {'ma'}, dimensions={0} | all-to-all | bytes 4194304 | tf_op jit(solution)/shard_map/all_to_all | solution.py:23
  279.7 2.1 copy.28
  (1 shorter events, 0.0 us)
Async XLA Ops:
  6.5 203.2 %all-gather.2.cloned.1.call-start = ((), (), s32[]{:S(2)}) async-start(), calls=%async_computation.2 | async-start | bytes 10485760 | tf_op jit(solution)/shard_map/all_gather | solution.py:17
  11.5 1.7 copy-start.1
  14.5 24.4 %copy-start = (bf16[2,768,2,512]{3,2,1,0:T(2,128)(2,1)S(1)}, bf16[2,768,2,512]{3,2,1,0:T(2,128)(2,1)}, u32[]{:S(2)}) copy-start(bf16[2,768,2,512]{3,2,1,0:T(2,128)(2,1)} %param.5) | copy-start | bytes 9437188
  38.8 5.4 %copy-start.6 = (s32[2]{0:T(128)S(1)}, s32[2]{0:T(128)}, u32[]{:S(2)}) copy-start(s32[2]{0:T(128)} %param.7) | copy-start | bytes 28
  38.8 5.5 %copy-start.2 = (bf16[2,1536,4,128]{1,3,2,0:T(8,128)(2,1)S(1)}, bf16[2,1536,4,128]{1,3,2,0:T(8,128)(2,1)}, u32[]{:S(2)}) copy-start(bf16[2,1536,4,128]{1,3,2,0:T(8,128)(2,1)} %copy-done.1) | copy-start | bytes 9437188
  38.8 5.5 %copy-start.5 = (bf16[2,768,512]{1,2,0:T(8,128)(2,1)S(1)}, bf16[2,768,512]{1,2,0:T(8,128)(2,1)}, u32[]{:S(2)}) copy-start(bf16[2,768,512]{1,2,0:T(8,128)(2,1)} %rev.3) | copy-start | bytes 4718596
  44.3 4.5 %copy-start.3 = (bf16[2,1536,4,128]{1,3,2,0:T(8,128)(2,1)S(1)}, bf16[2,1536,4,128]{1,3,2,0:T(8,128)(2,1)}, u32[]{:S(2)}) copy-start(bf16[2,1536,4,128]{1,3,2,0:T(8,128)(2,1)} %copy-done.1) | copy-start | bytes 9437188
  53.2 1.8 copy-start.4
Sparse Core Ops, SparseCore 0:
  123.1 86.5 all-gather.1
where the time goes:
time: 292 us; the launch traced here: 289 us
  blocking collectives  124 us (42%)
  waiting for transfers between devices  86.8 us (30%)
  local copies, waits for them, and re-layouts  49.1 us (17%)
  between operations  13.5 us (5%)
  matrix products  13.3 us (5%)
    all_gather x1, waiting for transfers between devices, radial_step(): lax.all_gather(separated, 'row', axis=5, tiled=True)  86.8 us
    all_to_all x1, blocking collectives, radial_step(): lax.all_to_all(coeff_block, 'ma', split_axis=2, concat_axis=0, tiled=True)  62.5 us
    all_to_all x1, blocking collectives, radial_step(): lax.all_to_all(returned, 'ma', split_axis=0, concat_axis=2, tiled=True)  61.4 us
    rev x1, local copies, waits for them, and re-layouts, per_device(): southern = flattened[:, half_theta:][:, ::-1].astype(jnp.float32)  24.4 us
    dot_general x1, matrix products, radial_step(): jnp.einsum('pjfrs,mpjfks->mpjfkr', inverse_part, lax.all_gather(separated...  6.91 us
    dot_general x2, matrix products, analyse(): jnp.einsum('mhj,mhx->mjx', table_part, chosen, preferred_element_type=jnp...  6.38 us
  transfers between devices with their start and end apart: 1, of which 1 were waited for; matrix products, arithmetic and copies ran while one was open for 0% of the time, Pallas kernels for 0%

commit v1 on v0

--- a/solution.py
+++ b/solution.py
@@ -1,26 +1,194 @@
 import jax
 import jax.numpy as jnp
 from jax import lax
+from jax.experimental import pallas as pl
+from jax.experimental.pallas import tpu as pltpu
 from jax.sharding import PartitionSpec as P
 
-
-def radial_step(coeff_block, inverse_part):
-    arrived = lax.all_to_all(coeff_block, "ma", split_axis=2, concat_axis=0, tiled=True)
-    order_total, parity_count, degree_block, part_count, radial_rows = arrived.shape
-    field_count = inverse_part.shape[2]
-    separated = arrived.reshape(
-        order_total, parity_count, degree_block, field_count, 2, radial_rows
-    )
-    summed = jnp.einsum(
-        "pjfrs,mpjfks->mpjfkr",
-        inverse_part,
-        lax.all_gather(separated, "row", axis=5, tiled=True),
-        preferred_element_type=jnp.float32,
-    )
-    returned = summed.astype(jnp.bfloat16).reshape(
-        order_total, parity_count, degree_block, part_count, radial_rows
-    )
-    return lax.all_to_all(returned, "ma", split_axis=0, concat_axis=2, tiled=True)
+MESH = pl.DeviceIdType.MESH
+RING = (4, 3, 5, 2, 6, 1, 7)
+ZN, ON, YN = 8, 8, 4
+SLOTS, PARITIES, HALVES = 2, 2, 2
+CHUNKS = PARITIES * HALVES
+ROWS, LANES = 16, 128
+
+
+def exchange_kernel(coef, inverse, out, held, gathered, solved, back, weights, zs, zr, ks, kr, ys, yr, ls, lr, ms, mr, own, load):
+    me = lax.axis_index("ma")
+    y = lax.axis_index("row")
+    z, o = me // ON, lax.rem(me, ON)
+
+    def z_peer(i):
+        return {"ma": lax.rem(z + i, ZN) * ON + o}
+
+    def o_peer(i):
+        return {"ma": z * ON + lax.rem(o + i, ON)}
+
+    def y_peer(i):
+        return {"row": lax.rem(y + i, YN)}
+
+    fetch = pltpu.make_async_copy(inverse, weights, load)
+    fetch.start()
+
+    barrier = pltpu.get_barrier_semaphore()
+    for i in range(1, ZN):
+        pl.semaphore_signal(barrier, inc=1, device_id=z_peer(i), device_id_type=MESH)
+        pl.semaphore_signal(barrier, inc=1, device_id=o_peer(i), device_id_type=MESH)
+    for i in (1, YN - 1):
+        pl.semaphore_signal(barrier, inc=1, device_id=y_peer(i), device_id_type=MESH)
+    pl.semaphore_wait(barrier, 2 * (ZN - 1) + 2)
+
+    def remote(src, dst, s, r, device):
+        return pltpu.make_async_remote_copy(src_ref=src, dst_ref=dst, send_sem=s, recv_sem=r, device_id=device, device_id_type=MESH)
+
+    def z_out(k, i):
+        p, h = k // HALVES, k % HALVES
+        there = lax.rem(z + i, ZN)
+        return remote(coef.at[:, p, pl.ds(there * ON, ON), h], held.at[k, z], zs.at[k, i], zr.at[k, i], z_peer(i))
+
+    def z_own(k):
+        p, h = k // HALVES, k % HALVES
+        return pltpu.make_async_copy(coef.at[:, p, pl.ds(z * ON, ON), h], held.at[k, z], own.at[0, k])
+
+    def o_out(k, i):
+        there = lax.rem(o + i, ON)
+        return remote(held.at[k, :, :, there], gathered.at[k, y, o], ks.at[k, i], kr.at[k, i], o_peer(i))
+
+    def o_own(k):
+        return pltpu.make_async_copy(held.at[k, :, :, o], gathered.at[k, y, o], own.at[1, k])
+
+    def y_first(k, i):
+        return remote(gathered.at[k, y], gathered.at[k, y], ys.at[k, i], yr.at[k, i], y_peer((1, YN - 1)[i]))
+
+    def y_second(k, i):
+        origin = lax.rem(y + (YN - 1, 1)[i], YN)
+        part = gathered.at[k, origin, pl.ds((0, ON // 2)[i], ON // 2)]
+        return remote(part, part, ys.at[k, 2 + i], yr.at[k, 2 + i], y_peer((1, YN - 1)[i]))
+
+    def l_out(k, i):
+        there = lax.rem(o + i, ON)
+        return remote(solved.at[k, there], back.at[k, :, :, o], ls.at[k, i], lr.at[k, i], o_peer(i))
+
+    def l_own(k):
+        return pltpu.make_async_copy(solved.at[k, o], back.at[k, :, :, o], own.at[2, k])
+
+    def m_out(k, i):
+        p, h = k // HALVES, k % HALVES
+        there = lax.rem(z + i, ZN)
+        return remote(back.at[k, there], out.at[:, p, pl.ds(z * ON, ON), h], ms.at[k, i], mr.at[k, i], z_peer(i))
+
+    def m_own(k):
+        p, h = k // HALVES, k % HALVES
+        return pltpu.make_async_copy(back.at[k, z], out.at[:, p, pl.ds(z * ON, ON), h], own.at[3, k])
+
+    def solve(k):
+        p, h = k // HALVES, k % HALVES
+        row = lax.broadcasted_iota(jnp.int32, (1, ROWS, LANES), 1)
+
+        @pl.loop(0, 2)
+        def _(half):
+            part = gathered[k, :, pl.ds(half * 4, 4)]
+            flat = part.reshape(YN, 4 * ZN * SLOTS * ROWS, LANES)
+            left = jnp.concatenate([flat[0], flat[1], flat[2], flat[3]], axis=1)
+            total = None
+            for jl in range(4):
+                right = weights[p, h * 4 + jl].reshape(2 * LANES, YN * LANES)
+                product = lax.dot_general(left, right, (((1,), (1,)), ((), ())), preferred_element_type=jnp.float32)
+                product = product.reshape(4 * ZN * SLOTS, ROWS, 2 * LANES)
+                for f in range(2):
+                    piece = product[:, :, f * LANES:(f + 1) * LANES]
+                    piece = jnp.where(row // 2 == jl * 2 + f, piece, 0.0)
+                    total = piece if total is None else total + piece
+            solved[k, pl.ds(half * 4, 4)] = total.astype(jnp.bfloat16).reshape(4, ZN, SLOTS, ROWS, LANES)
+
+    for k in range(CHUNKS):
+        for i in RING:
+            z_out(k, i).start()
+        z_own(k).start()
+
+    def stage_o(k):
+        z_own(k).wait()
+        for i in range(1, ZN):
+            z_out(k, i).wait_recv()
+        for i in range(1, ON):
+            o_out(k, i).start()
+        o_own(k).start()
+
+    def stage_y(k):
+        o_own(k).wait()
+        for i in range(1, ON):
+            o_out(k, i).wait_recv()
+        for i in range(2):
+            y_first(k, i).start()
+
+    def stage_f(k):
+        for i in range(2):
+            y_first(k, i).wait_recv()
+            y_second(k, i).start()
+
+    def stage_s(k):
+        if k == 0:
+            fetch.wait()
+        for i in range(2):
+            y_second(k, i).wait_recv()
+        solve(k)
+        for i in range(1, ON):
+            l_out(k, i).start()
+        l_own(k).start()
+
+    def stage_m(k):
+        l_own(k).wait()
+        for i in range(1, ON):
+            l_out(k, i).wait_recv()
+        for i in RING:
+            m_out(k, i).start()
+        m_own(k).start()
+
+    stages = (stage_o, stage_y, stage_f, stage_s, stage_m)
+    for step in range(CHUNKS + len(stages) - 1):
+        for n, stage in enumerate(stages):
+            if 0 <= step - n < CHUNKS:
+                stage(step - n)
+
+    for k in range(CHUNKS):
+        m_own(k).wait()
+        for i in range(1, ZN):
+            m_out(k, i).wait_recv()
+    for k in range(CHUNKS):
+        for i in range(1, ZN):
+            z_out(k, i).wait_send()
+            o_out(k, i).wait_send()
+            l_out(k, i).wait_send()
+            m_out(k, i).wait_send()
+        for i in range(2):
+            y_first(k, i).wait_send()
+            y_second(k, i).wait_send()
+
+
+def exchange(coef, inverse):
+    tile = (ROWS, LANES)
+    dma = pltpu.SemaphoreType.DMA
+    return pl.pallas_call(
+        exchange_kernel,
+        out_shape=jax.ShapeDtypeStruct(coef.shape, coef.dtype),
+        in_specs=[pl.BlockSpec(memory_space=pl.ANY)] * 2,
+        out_specs=pl.BlockSpec(memory_space=pl.ANY),
+        scratch_shapes=[
+            pltpu.VMEM((CHUNKS, ZN, SLOTS, ON) + tile, jnp.bfloat16),
+            pltpu.VMEM((CHUNKS, YN, ON, ZN, SLOTS) + tile, jnp.bfloat16),
+            pltpu.VMEM((CHUNKS, ON, ZN, SLOTS) + tile, jnp.bfloat16),
+            pltpu.VMEM((CHUNKS, ZN, SLOTS, ON) + tile, jnp.bfloat16),
+            pltpu.VMEM(inverse.shape, jnp.bfloat16),
+            dma((CHUNKS, ZN)), dma((CHUNKS, ZN)),
+            dma((CHUNKS, ON)), dma((CHUNKS, ON)),
+            dma((CHUNKS, 4)), dma((CHUNKS, 4)),
+            dma((CHUNKS, ON)), dma((CHUNKS, ON)),
+            dma((CHUNKS, ZN)), dma((CHUNKS, ZN)),
+            dma((4, CHUNKS)),
+            dma,
+        ],
+        compiler_params=pltpu.CompilerParams(collective_id=0, has_side_effects=True, vmem_limit_bytes=48 * 1024 * 1024),
+    )(coef, inverse)
 
 
 def per_device(nonlinear, legendre, inverse, orders):
@@ -45,7 +213,8 @@
         )
 
     coefficients = jnp.concatenate([analyse(0), analyse(1)], axis=1)
-    return radial_step(coefficients, inverse)
+    coef = coefficients.reshape(SLOTS, PARITIES, ZN * ON, HALVES, ROWS, LANES)
+    return exchange(coef, inverse).reshape(coefficients.shape)
 
 
 def solution(mesh):

time: 292 us -> 185 us (0.63)
  Pallas kernels: 0 us -> 139 us
  blocking collectives: 124 us -> 0 us
  waiting for transfers between devices: 86.8 us -> 0 us
  between operations: 13.5 us -> 0.11 us
  matrix products: 13.3 us -> 2.07 us
  local copies, waits for them, and re-layouts: 49.1 us -> 39.7 us
    pallas_call x0 -> x1, Pallas kernels: none -> 139 us  [exchange(): pl.pallas_call(exchange_kernel, out_shape=jax.ShapeDtypeStruct(coef.shape...]
    all_to_all x2 -> x0, blocking collectives: 124 us -> none  [the longest x1 62.5 us: radial_step(): lax.all_to_all(coeff_block, 'ma', split_axis=2, concat_axis=0, tiled=True)]
    all_gather x1 -> x0, waiting for transfers between devices: 86.8 us -> none  [radial_step(): lax.all_gather(separated, 'row', axis=5, tiled=True)]
    dot_general x1 -> x0, matrix products: 6.91 us -> none  [radial_step(): jnp.einsum('pjfrs,mpjfks->mpjfkr', inverse_part, lax.all_gather(separated...]
    all_to_all x3 -> x0, local copies, waits for them, and re-layouts: 6.16 us -> none  [the longest x2 4.04 us: radial_step(): lax.all_to_all(coeff_block, 'ma', split_axis=2, concat_axis=0, tiled=True)]
    reshape x3 -> x0, local copies, waits for them, and re-layouts: 5.89 us -> none  [the longest x2 4.27 us: analyse(): product.astype(jnp.bfloat16)]
    dot_general x2, matrix products: 6.38 us -> 2.07 us  [analyse(): jnp.einsum('mhj,mhx->mjx', table_part, chosen, preferred_element_type=jnp...]
  transfers between devices with their start and end apart: 1 -> 0, of which waited for: 1 -> 0; matrix products, arithmetic and copies ran while one was open for 0% -> 0% of each run, Pallas kernels for 0% -> 0%
where the time goes in v1:
time: 185 us; the launch traced here: 182 us
  Pallas kernels  139 us (75%)
  local copies, waits for them, and re-layouts  39.7 us (21%)
  matrix products  2.07 us (1%)
    pallas_call x1, Pallas kernels, exchange(): pl.pallas_call(exchange_kernel, out_shape=jax.ShapeDtypeStruct(coef.shape...  139 us
    rev x1, local copies, waits for them, and re-layouts, per_device(): southern = flattened[:, half_theta:][:, ::-1].astype(jnp.float32)  24.3 us
    slice x1, local copies, waits for them, and re-layouts, analyse(): table_part = legendre[:, :, parity, :]  4.47 us
    reshape x1, local copies, waits for them, and re-layouts, per_device(): nonlinear.reshape(order_count, theta_count, part_count * radial_rows)  4.32 us

profile of v1, /device:TPU:1, one launch (start us, length us, event | category | flops | bytes accessed | tf_op | source)
XLA Modules:
  0.0 182.3 jit_solution(8529752146444288010)
XLA Ops:
  0.0 0.7 fusion.16
  0.7 0.7 broadcast_compare_fusion.1
  1.4 4.3 %copy.11 = bf16[2,1536,4,128]{1,3,2,0:T(8,128)(2,1)S(1)} copy(bf16[2,1536,4,128]{3,2,1,0:T(4,128)(2,1)} %param.4) | data formatting | bytes 6291456 | tf_op jit(solution)/shard_map/reshape | solution.py:198
  5.7 0.0 copy-start.1
  5.8 1.6 copy-done.1
  7.4 1.2 slice.17
  8.6 0.0 copy-start
  8.6 24.3 %rev.3 = bf16[2,768,512]{1,2,0:T(8,128)(2,1)} reverse(bf16[2,768,512]{1,2,0:T(8,128)(2,1)} %slice.17), dimensions={1} | reverse | bytes 3145728 | tf_op jit(solution)/shard_map/rev | solution.py:200
  32.9 0.0 copy-done
  32.9 0.0 copy-start.2
  32.9 0.0 copy-start.3
  32.9 4.5 %fusion.20 = (bf16[2,768,1,512]{3,2,1,0:T(2,128)(2,1)S(1)}, bf16[2,768,1,512]{3,2,1,0:T(2,128)(2,1)S(1)}) fusion(bf16[2,768,2,512]{3,2,1,0:T(2,128)(2,1)S(1)} %copy-done), kind=kLoop, calls=%fused_computation.29 | loop fusion | bytes 6291456 | tf_op jit(solution)/shard_map/slice | solution.py:207
  37.4 0.0 copy-done.2
  37.4 0.0 copy-done.3
  37.4 1.0 fusion.6
  38.5 1.0 fusion.9
  39.5 0.5 copy.10
  40.1 0.7 concatenate.9
  40.8 0.5 copy.8
  41.3 0.7 concatenate.8
  42.0 0.2 pad_maximum_fusion.coef
  42.2 138.8 %shard_map.46 = bf16[2,2,64,2,16,128]{5,4,3,2,1,0:T(8,128)(2,1)S(1)} custom-call(bf16[2,2,64,2,16,128]{5,4,3,2,1,0:T(8,128)(2,1)S(1)} %pad_maximum_fusion.coef, bf16[2,8,2,128,512]{4,3,2,1,0:T(8,128)(2,1)} %inverse.1), custom_call_target="tpu_custom_call" | custom-call | tf_op jit(solution)/shard_map/pallas_call | solution.py:171
  181.0 1.3 copy.23
  (1 shorter events, 0.0 us)
Async XLA Ops:
  5.7 1.6 copy-start.1
  8.6 24.3 %copy-start = (bf16[2,768,2,512]{3,2,1,0:T(2,128)(2,1)S(1)}, bf16[2,768,2,512]{3,2,1,0:T(2,128)(2,1)}, u32[]{:S(2)}) copy-start(bf16[2,768,2,512]{3,2,1,0:T(2,128)(2,1)} %param.5) | copy-start | bytes 9437188
  32.9 4.5 %copy-start.2 = (bf16[2,1536,4,128]{1,3,2,0:T(8,128)(2,1)S(1)}, bf16[2,1536,4,128]{1,3,2,0:T(8,128)(2,1)}, u32[]{:S(2)}) copy-start(bf16[2,1536,4,128]{1,3,2,0:T(8,128)(2,1)} %copy-done.1) | copy-start | bytes 9437188
  32.9 4.5 %copy-start.3 = (bf16[2,768,512]{1,2,0:T(8,128)(2,1)S(1)}, bf16[2,768,512]{1,2,0:T(8,128)(2,1)}, u32[]{:S(2)}) copy-start(bf16[2,768,512]{1,2,0:T(8,128)(2,1)} %rev.3) | copy-start | bytes 4718596

commit v2 on v1

v2 whole, which is shorter than its diff:
```python
import jax
import jax.numpy as jnp
from jax import lax
from jax.experimental import pallas as pl
from jax.experimental.pallas import tpu as pltpu
from jax.sharding import PartitionSpec as P

MESH = pl.DeviceIdType.MESH
RING = (4, 3, 5, 2, 6, 1, 7)
ZN, ON, YN = 8, 8, 4
SLOTS, PARITIES, HALVES, QUAD = 2, 2, 2, 4
PER_SLOT = PARITIES * HALVES
CHUNKS = SLOTS * PER_SLOT
ROWS, LANES = 16, 128
PARTS = 4
THETA, FOLD = 768, 256
DEGREES = 512
BLOCKS = DEGREES // LANES


def kernel(orders, nonlinear, legendre, inverse, out,
           raw, wide, folded, table, stage, coef, held, gathered, solved, back, weights, zeros,
           zs, zr, ks, kr, ys, yr, ls, lr, ms, mr, own, load, fill):
    me = lax.axis_index("ma")
    y = lax.axis_index("row")
    z, o = me // ON, lax.rem(me, ON)
    upper = z >= ZN // 2

    def z_peer(i):
        return {"ma": lax.rem(z + i, ZN) * ON + o}

    def o_peer(i):
        return {"ma": z * ON + lax.rem(o + i, ON)}

    def y_peer(i):
        return {"row": lax.rem(y + i, YN)}

    fetches = []
    for slot in range(SLOTS):
        fetches.append(pltpu.make_async_copy(nonlinear.at[slot], raw.at[slot, 0], load.at[2 * slot]))
        fetches.append(pltpu.make_async_copy(legendre.at[slot], raw.at[slot, 1], load.at[2 * slot + 1]))
    fetches.append(pltpu.make_async_copy(inverse, weights, load.at[2 * SLOTS]))
    for fetch in fetches:
        fetch.start()

    barrier = pltpu.get_barrier_semaphore()
    for i in range(1, ZN):
        pl.semaphore_signal(barrier, inc=1, device_id=z_peer(i), device_id_type=MESH)
        pl.semaphore_signal(barrier, inc=1, device_id=o_peer(i), device_id_type=MESH)
    for i in (1, YN - 1):
        pl.semaphore_signal(barrier, inc=1, device_id=y_peer(i), device_id_type=MESH)

    def remote(src, dst, s, r, device):
        return pltpu.make_async_remote_copy(src_ref=src, dst_ref=dst, send_sem=s, recv_sem=r, device_id=device, device_id_type=MESH)

    def where(k):
        inner = k % PER_SLOT
        return k // PER_SLOT, inner // HALVES, inner % HALVES

    def z_out(k, i):
        slot, p, h = where(k)
        there = lax.rem(z + i, ZN)
        return remote(coef.at[slot, p, pl.ds(there * ON, ON), h], held.at[k, z], zs.at[k, i], zr.at[k, i], z_peer(i))

    def z_own(k):
        slot, p, h = where(k)
        return pltpu.make_async_copy(coef.at[slot, p, pl.ds(z * ON, ON), h], held.at[k, z], own.at[0, k])

    def o_out(k, i):
        there = lax.rem(o + i, ON)
        return remote(held.at[k, :, there], gathered.at[k, y, o], ks.at[k, i], kr.at[k, i], o_peer(i))

    def o_own(k):
        return pltpu.make_async_copy(held.at[k, :, o], gathered.at[k, y, o], own.at[1, k])

    def y_first(k, i):
        return remote(gathered.at[k, y], gathered.at[k, y], ys.at[k, i], yr.at[k, i], y_peer((1, YN - 1)[i]))

    def y_second(k, i):
        origin = lax.rem(y + (YN - 1, 1)[i], YN)
        part = gathered.at[k, origin, pl.ds((0, ON // 2)[i], ON // 2)]
        return remote(part, part, ys.at[k, 2 + i], yr.at[k, 2 + i], y_peer((1, YN - 1)[i]))

    def l_out(k, i):
        there = lax.rem(o + i, ON)
        return remote(solved.at[k, there], back.at[k, :, o], ls.at[k, i], lr.at[k, i], o_peer(i))

    def l_own(k):
        return pltpu.make_async_copy(solved.at[k, o], back.at[k, :, o], own.at[2, k])

    def m_out(k, i):
        slot, p, h = where(k)
        there = lax.rem(z + i, ZN)
        return remote(back.at[k, there], out.at[slot, p, pl.ds(z * ON, ON), h], ms.at[k, i], mr.at[k, i], z_peer(i))

    def m_own(k):
        slot, p, h = where(k)
        return pltpu.make_async_copy(back.at[k, z], out.at[slot, p, pl.ds(z * ON, ON), h], own.at[3, k])

    def fold(slot):
        fetches[2 * slot].wait()
        wide[...] = raw[slot, 0].astype(jnp.float32)
        index = lax.broadcasted_iota(jnp.int32, (FOLD, FOLD), 0) + lax.broadcasted_iota(jnp.int32, (FOLD, FOLD), 1)
        flip = (index == FOLD - 1).astype(jnp.bfloat16)
        sign = jnp.where(orders[slot] % 2 == 0, 1.0, -1.0).astype(jnp.float32)

        def rows(block):
            return [wide[pl.ds(block * FOLD * PARTS + c, FOLD, stride=PARTS), :] for c in range(PARTS)]

        for b in range(THETA // FOLD):
            north = jnp.concatenate(rows(b), axis=1)
            south = jnp.concatenate([v.astype(jnp.bfloat16) for v in rows(2 * THETA // FOLD - 1 - b)], axis=1)
            south = jnp.dot(flip, south, preferred_element_type=jnp.float32) * sign
            folded[0, b * FOLD:(b + 1) * FOLD, :] = (north + south).astype(jnp.bfloat16)
            folded[1, b * FOLD:(b + 1) * FOLD, :] = (north - south).astype(jnp.bfloat16)

    def tabulate(slot):
        fetches[2 * slot + 1].wait()
        wide[...] = raw[slot, 1].astype(jnp.float32)
        for p in range(PARITIES):
            for b in range(BLOCKS):
                table[p, :, b * LANES:(b + 1) * LANES] = wide[pl.ds(b * PARITIES + p, THETA, stride=BLOCKS * PARITIES), :].astype(jnp.bfloat16)

    def analyse(slot, p):
        product = lax.dot_general(table[p], folded[p], (((0,), (0,)), ((), ())), preferred_element_type=jnp.float32)
        degree = 2 * lax.broadcasted_iota(jnp.int32, (DEGREES, 1), 0) + p
        product = jnp.where(degree >= orders[slot], product, 0.0)
        for c in range(PARTS):
            stage[pl.ds(c, DEGREES, stride=PARTS), :] = product[:, c * LANES:(c + 1) * LANES]
        coef[slot, p] = stage[...].astype(jnp.bfloat16).reshape(ZN * ON, HALVES, ROWS, LANES)

    def solve(k):
        slot, p, h = where(k)
        row = lax.broadcasted_iota(jnp.int32, (1, ROWS, LANES), 1)
        flat = gathered[k].reshape(YN, ON * ZN * ROWS, LANES)
        left = jnp.concatenate([flat[n] for n in range(YN)], axis=1)
        total = None
        for jl in range(QUAD):
            right = weights[p, h * QUAD + jl].reshape(2 * LANES, YN * LANES)
            product = lax.dot_general(left, right, (((1,), (1,)), ((), ())), preferred_element_type=jnp.float32)
            product = product.reshape(ON * ZN, ROWS, 2 * LANES)
            for f in range(2):
                piece = product[:, :, f * LANES:(f + 1) * LANES]
                total = piece if total is None else jnp.where(row // 2 == jl * 2 + f, piece, total)
        solved[k] = total.astype(jnp.bfloat16).reshape(ON, ZN, ROWS, LANES)

    def stage_z(k):
        slot = k // PER_SLOT
        for i in RING:
            if slot == 0:
                z_out(k, i).start()
            else:
                @pl.when(lax.rem(z + i, ZN) >= ZN // 2)
                def _():
                    z_out(k, i).start()
        if slot == 0:
            z_own(k).start()
        else:
            @pl.when(upper)
            def _():
                z_own(k).start()

    def stage_o(k):
        z_own(k).wait()
        for i in range(1, ZN):
            z_out(k, i).wait_recv()
        for i in range(1, ON):
            o_out(k, i).start()
        o_own(k).start()

    def stage_y(k):
        o_own(k).wait()
        for i in range(1, ON):
            o_out(k, i).wait_recv()
        for i in range(2):
            y_first(k, i).start()

    def stage_f(k):
        for i in range(2):
            y_first(k, i).wait_recv()
            y_second(k, i).start()

    def stage_s(k):
        for i in range(1, ON):
            o_out(k, i).wait_send()
        for i in range(2):
            y_second(k, i).wait_recv()
        solve(k)
        for i in range(1, ON):
            l_out(k, i).start()
        l_own(k).start()

    def stage_m(k):
        for i in range(2):
            y_first(k, i).wait_send()
            y_second(k, i).wait_send()
        l_own(k).wait()
        for i in range(1, ON):
            l_out(k, i).wait_recv()
        for i in RING:
            m_out(k, i).start()
        m_own(k).start()

    fold(0)
    tabulate(0)
    analyse(0, 0)
    pl.semaphore_wait(barrier, 2 * (ZN - 1) + 2)
    stage_z(0)
    stage_z(1)
    analyse(0, 1)
    stage_z(2)
    stage_z(3)
    zeros[...] = jnp.zeros_like(zeros)
    fills = [pltpu.make_async_copy(zeros, out.at[1, n // HALVES, pl.ds(0, ZN * ON // 2), n % HALVES], fill.at[n]) for n in range(PER_SLOT)]
    for copy in fills:
        copy.start()
    fold(1)
    tabulate(1)
    stage_o(0)
    analyse(1, 0)
    stage_z(4)
    stage_z(5)
    analyse(1, 1)
    stage_z(6)
    stage_z(7)
    fetches[2 * SLOTS].wait()

    @pl.loop(0, CHUNKS + 3)
    def _(step):
        for stage_of, lag in ((stage_y, 0), (stage_o, -1), (stage_f, 1), (stage_s, 2), (stage_m, 3)):
            k = step - lag
            valid = jnp.logical_and(k >= 0, k < CHUNKS)
            live = jnp.logical_or(k < PER_SLOT, upper)

            @pl.when(jnp.logical_and(valid, live))
            def _():
                stage_of(k)

    for copy in fills:
        copy.wait()
    for k in range(CHUNKS):
        slot = k // PER_SLOT

        def sent():
            for i in range(1, ON):
                l_out(k, i).wait_send()
                m_out(k, i).wait_send()

        if slot == 0:
            for i in range(1, ZN):
                z_out(k, i).wait_send()
            sent()
        else:
            for i in range(1, ZN):
                @pl.when(lax.rem(z + i, ZN) >= ZN // 2)
                def _():
                    z_out(k, i).wait_send()
            pl.when(upper)(sent)
    for k in range(CHUNKS):
        if k < PER_SLOT:
            m_own(k).wait()
            for i in range(1, ZN):
                m_out(k, i).wait_recv()
        else:
            @pl.when(upper)
            def _():
                m_own(k).wait()
            for i in range(1, ZN):
                @pl.when(lax.rem(z + ZN - i, ZN) >= ZN // 2)
                def _():
                    m_out(k, i).wait_recv()


def per_device(nonlinear, legendre, inverse, orders):
    tile = (ROWS, LANES)
    dma = pltpu.SemaphoreType.DMA
    field = nonlinear.reshape(SLOTS, 2 * THETA * PARTS, LANES)
    values = legendre.reshape(SLOTS, THETA, PARITIES, BLOCKS, LANES).transpose(0, 1, 3, 2, 4)
    values = values.reshape(SLOTS, THETA * BLOCKS * PARITIES, LANES)
    solved = pl.pallas_call(
        kernel,
        out_shape=jax.ShapeDtypeStruct((SLOTS, PARITIES, ZN * ON, HALVES) + tile, jnp.bfloat16),
        in_specs=[pl.BlockSpec(memory_space=pltpu.SMEM)] + [pl.BlockSpec(memory_space=pl.ANY)] * 3,
        out_specs=pl.BlockSpec(memory_space=pl.ANY),
        scratch_shapes=[
            pltpu.VMEM((SLOTS, 2) + field.shape[1:], jnp.bfloat16),
            pltpu.VMEM(field.shape[1:], jnp.float32),
            pltpu.VMEM((PARITIES, THETA, PARTS * LANES), jnp.bfloat16),
            pltpu.VMEM((PARITIES, THETA, DEGREES), jnp.bfloat16),
            pltpu.VMEM((DEGREES * PARTS, LANES), jnp.float32),
            pltpu.VMEM((SLOTS, PARITIES, ZN * ON, HALVES) + tile, jnp.bfloat16),
            pltpu.VMEM((CHUNKS, ZN, ON) + tile, jnp.bfloat16),
            pltpu.VMEM((CHUNKS, YN, ON, ZN) + tile, jnp.bfloat16),
            pltpu.VMEM((CHUNKS, ON, ZN) + tile, jnp.bfloat16),
            pltpu.VMEM((CHUNKS, ZN, ON) + tile, jnp.bfloat16),
            pltpu.VMEM(inverse.shape, jnp.bfloat16),
            pltpu.VMEM((ZN * ON // 2,) + tile, jnp.bfloat16),
            dma((CHUNKS, ZN)), dma((CHUNKS, ZN)),
            dma((CHUNKS, ON)), dma((CHUNKS, ON)),
            dma((CHUNKS, 4)), dma((CHUNKS, 4)),
            dma((CHUNKS, ON)), dma((CHUNKS, ON)),
            dma((CHUNKS, ZN)), dma((CHUNKS, ZN)),
            dma((4, CHUNKS)),
            dma((2 * SLOTS + 1,)),
            dma((PER_SLOT,)),
        ],
        compiler_params=pltpu.CompilerParams(collective_id=0, has_side_effects=True, vmem_limit_bytes=52 * 1024 * 1024),
    )(orders, field, values, inverse)
    return solved.reshape(SLOTS, PARITIES, DEGREES, PARTS, LANES)


def solution(mesh):
    in_specs = (
        P("ma", None, None, "row"),
        P("ma", None, None, None),
        P(None, "ma", None, "row", None),
        P("ma"),
    )
    out_specs = P("ma", None, None, None, "row")
    return jax.shard_map(
        per_device, mesh=mesh, in_specs=in_specs, out_specs=out_specs, check_vma=False
    )
```

time: 185 us -> 127 us (0.69); the launches traced: 182 us -> 127 us
  local copies, waits for them, and re-layouts: 39.7 us -> 4.28 us
  Pallas kernels: 139 us -> 123 us
  matrix products: 2.07 us -> 0 us
    rev x1 -> x0, local copies, waits for them, and re-layouts: 24.3 us -> none  [per_device(): southern = flattened[:, half_theta:][:, ::-1].astype(jnp.float32)]
    pallas_call x1, Pallas kernels: 139 us -> 123 us  [per_device(): pl.pallas_call(kernel, out_shape=jax.ShapeDtypeStruct((SLOTS, PARITIES, Z...]
    slice x2 -> x0, local copies, waits for them, and re-layouts: 5.71 us -> none  [the longest x1 4.47 us: analyse(): table_part = legendre[:, :, parity, :]]
    reshape x1 -> x0, local copies, waits for them, and re-layouts: 4.32 us -> none  [per_device(): nonlinear.reshape(order_count, theta_count, part_count * radial_rows)]
    dot_general x2 -> x0, matrix products: 2.07 us -> none  [analyse(): jnp.einsum('mhj,mhx->mjx', table_part, chosen, preferred_element_type=jnp...]
    unnamed x9 -> x3, local copies, waits for them, and re-layouts: 2.97 us -> 4.28 us
where the time goes in v2:
time: 127 us
  Pallas kernels  123 us (97%)
  local copies, waits for them, and re-layouts  4.28 us (3%)
    pallas_call x1, Pallas kernels, per_device(): pl.pallas_call(kernel, out_shape=jax.ShapeDtypeStruct((SLOTS, PARITIES, Z...  123 us
    unnamed x3, local copies, waits for them, and re-layouts  4.28 us

profile of v2, /device:TPU:1, one launch (start us, length us, event | category | flops | bytes accessed | tf_op | source)
XLA Modules:
  0.0 127.1 jit_solution(17362089146624325086)
XLA Ops:
  0.0 0.0 copy-start
  0.0 0.7 copy-done
  0.7 122.8 %shard_map.46 = bf16[2,2,64,2,16,128]{5,4,3,2,1,0:T(8,128)(2,1)} custom-call(s32[2]{0:T(128)S(1)} %copy-done, bf16[2,6144,128]{2,1,0:T(8,128)(2,1)} %bitcast.8, bf16[2,6144,128]{2,1,0:T(8,128)(2,1)} %bitcast.9, bf16[2,8,2,128,512]{4,3,2,1,0:T(8,128)(2,1)} %inverse.1), custom_call_target="tpu_custom_call" | custom-call | tf_op jit(solution)/shard_map/pallas_call | solution.py:280
  123.4 3.6 %copy.7 = bf16[2,2,512,4,128]{4,3,2,1,0:T(4,128)(2,1)} copy(bf16[2,2,512,4,128]{4,3,2,1,0:T(4,128)(2,1)} %bitcast.7) | data formatting | bytes 4194304
Async XLA Ops:
  0.0 0.7 copy-start

commit v3 on v2

v3 whole, which is shorter than its diff:
```python
import jax
import jax.numpy as jnp
from jax import lax
from jax.experimental import pallas as pl
from jax.experimental.pallas import tpu as pltpu
from jax.sharding import PartitionSpec as P

MESH = pl.DeviceIdType.MESH
RING = (4, 3, 5, 2, 6, 1, 7)
ZN, ON, YN = 8, 8, 4
MA = ZN * ON
SLOTS, PARITIES, HALVES, QUAD = 2, 2, 2, 4
PER_SLOT = PARITIES * HALVES
CHUNKS = SLOTS * PER_SLOT
ROWS, LANES = 16, 128
Z_AHEAD, F_LAG, S_LAG = 4, 1, 2
PARTS = 4
THETA, FOLD = 768, 256
DEGREES = 512
BLOCKS = DEGREES // LANES


def kernel(orders, nonlinear, legendre, inverse, out,
           raw, wide, folded, table, stage, coef, gathered, solved, weights, zeros,
           zs, zr, ys, yr, ms, mr, own, load, fill):
    me = lax.axis_index("ma")
    y = lax.axis_index("row")
    z, o = me // ON, lax.rem(me, ON)
    upper = z >= ZN // 2

    def y_peer(i):
        return {"row": lax.rem(y + i, YN)}

    fetches = []
    for slot in range(SLOTS):
        fetches.append(pltpu.make_async_copy(nonlinear.at[slot], raw.at[slot, 0], load.at[2 * slot]))
        fetches.append(pltpu.make_async_copy(legendre.at[slot], raw.at[slot, 1], load.at[2 * slot + 1]))
    fetches.append(pltpu.make_async_copy(inverse, weights, load.at[2 * SLOTS]))
    for fetch in fetches:
        fetch.start()

    barrier = pltpu.get_barrier_semaphore()

    @pl.loop(1, MA)
    def _(i):
        pl.semaphore_signal(barrier, inc=1, device_id={"ma": lax.rem(me + i, MA)}, device_id_type=MESH)

    for i in (1, YN - 1):
        pl.semaphore_signal(barrier, inc=1, device_id=y_peer(i), device_id_type=MESH)

    def remote(src, dst, s, r, device):
        return pltpu.make_async_remote_copy(src_ref=src, dst_ref=dst, send_sem=s, recv_sem=r, device_id=device, device_id_type=MESH)

    def where(k):
        inner = k % PER_SLOT
        return k // PER_SLOT, inner // HALVES, inner % HALVES

    def z_out(k, there):
        slot, p, h = where(k)
        return remote(coef.at[slot, p, there, h], gathered.at[k, y, me], zs.at[k], zr.at[k], {"ma": there})

    def z_own(k):
        slot, p, h = where(k)
        return pltpu.make_async_copy(coef.at[slot, p, me, h], gathered.at[k, y, me], own.at[0, k])

    def y_first(k, i):
        return remote(gathered.at[k, y], gathered.at[k, y], ys.at[k, i], yr.at[k, i], y_peer((1, YN - 1)[i]))

    def y_second(k, i):
        origin = lax.rem(y + (YN - 1, 1)[i], YN)
        part = gathered.at[k, origin, pl.ds((0, MA // 2)[i], MA // 2)]
        return remote(part, part, ys.at[k, 2 + i], yr.at[k, 2 + i], y_peer((1, YN - 1)[i]))

    def m_out(k, there):
        slot, p, h = where(k)
        return remote(solved.at[k, there], out.at[slot, p, me, h], ms.at[k], mr.at[k], {"ma": there})

    def m_own(k):
        slot, p, h = where(k)
        return pltpu.make_async_copy(solved.at[k, me], out.at[slot, p, me, h], own.at[1, k])

    def drain(sem, count):
        part = solved.at[0, pl.ds(0, count)]
        pltpu.make_async_copy(part, part, sem).wait()

    def to_all(copy, k):
        @pl.loop(0, ON)
        def _(i):
            beside = lax.rem(o + i, ON)
            for n in RING:
                copy(k, lax.rem(z + n, ZN) * ON + beside).start()

            @pl.when(i > 0)
            def _():
                copy(k, z * ON + beside).start()

    def to_upper(copy, k):
        @pl.loop(0, ON)
        def _(i):
            beside = lax.rem(o + i, ON)
            for n in range(ZN // 2):
                there = (ZN // 2 + lax.rem(z + n, ZN // 2)) * ON + beside

                @pl.when(there != me)
                def _():
                    copy(k, there).start()

    def fold(slot):
        fetches[2 * slot].wait()
        wide[...] = raw[slot, 0].astype(jnp.float32)
        index = lax.broadcasted_iota(jnp.int32, (FOLD, FOLD), 0) + lax.broadcasted_iota(jnp.int32, (FOLD, FOLD), 1)
        flip = (index == FOLD - 1).astype(jnp.bfloat16)
        sign = jnp.where(orders[slot] % 2 == 0, 1.0, -1.0).astype(jnp.float32)

        def rows(block):
            return [wide[pl.ds(block * FOLD * PARTS + c, FOLD, stride=PARTS), :] for c in range(PARTS)]

        for b in range(THETA // FOLD):
            north = jnp.concatenate(rows(b), axis=1)
            south = jnp.concatenate([v.astype(jnp.bfloat16) for v in rows(2 * THETA // FOLD - 1 - b)], axis=1)
            south = jnp.dot(flip, south, preferred_element_type=jnp.float32) * sign
            folded[0, b * FOLD:(b + 1) * FOLD, :] = (north + south).astype(jnp.bfloat16)
            folded[1, b * FOLD:(b + 1) * FOLD, :] = (north - south).astype(jnp.bfloat16)

    def tabulate(slot):
        fetches[2 * slot + 1].wait()
        wide[...] = raw[slot, 1].astype(jnp.float32)
        for p in range(PARITIES):
            for b in range(BLOCKS):
                table[p, :, b * LANES:(b + 1) * LANES] = wide[pl.ds(b * PARITIES + p, THETA, stride=BLOCKS * PARITIES), :].astype(jnp.bfloat16)

    def analyse(slot, p):
        product = lax.dot_general(table[p], folded[p], (((0,), (0,)), ((), ())), preferred_element_type=jnp.float32)
        degree = 2 * lax.broadcasted_iota(jnp.int32, (DEGREES, 1), 0) + p
        product = jnp.where(degree >= orders[slot], product, 0.0)
        for c in range(PARTS):
            stage[pl.ds(c, DEGREES, stride=PARTS), :] = product[:, c * LANES:(c + 1) * LANES]
        coef[slot, p] = stage[...].astype(jnp.bfloat16).reshape(MA, HALVES, ROWS, LANES)

    def solve(k):
        slot, p, h = where(k)
        row = lax.broadcasted_iota(jnp.int32, (1, ROWS, LANES), 1)
        flat = gathered[k].reshape(YN, MA * ROWS, LANES)
        left = jnp.concatenate([flat[n] for n in range(YN)], axis=1)
        total = None
        for jl in range(QUAD):
            right = weights[p, h * QUAD + jl].reshape(2 * LANES, YN * LANES)
            product = lax.dot_general(left, right, (((1,), (1,)), ((), ())), preferred_element_type=jnp.float32)
            product = product.reshape(MA, ROWS, 2 * LANES)
            for f in range(2):
                piece = product[:, :, f * LANES:(f + 1) * LANES]
                total = piece if total is None else jnp.where(row // 2 == jl * 2 + f, piece, total)
        solved[k] = total.astype(jnp.bfloat16).reshape(MA, ROWS, LANES)

    def stage_z(k):
        @pl.when(k < PER_SLOT)
        def _():
            to_all(z_out, k)
            z_own(k).start()

        @pl.when(k >= PER_SLOT)
        def _():
            to_upper(z_out, k)

            @pl.when(upper)
            def _():
                z_own(k).start()

    def stage_y(k):
        z_own(k).wait()
        drain(zr.at[k], MA - 1)
        for i in range(2):
            y_first(k, i).start()

    def stage_f(k):
        for i in range(2):
            y_first(k, i).wait_recv()
            y_second(k, i).start()

    def stage_s(k):
        for i in range(2):
            y_second(k, i).wait_recv()
        solve(k)
        to_all(m_out, k)
        m_own(k).start()

    fold(0)
    tabulate(0)
    analyse(0, 0)
    pl.semaphore_wait(barrier, MA - 1 + 2)
    stage_z(0)
    stage_z(1)
    analyse(0, 1)
    for k in range(2, Z_AHEAD):
        stage_z(k)
    zeros[...] = jnp.zeros_like(zeros)
    fills = [pltpu.make_async_copy(zeros, out.at[1, n // HALVES, pl.ds(0, MA // 2), n % HALVES], fill.at[n]) for n in range(PER_SLOT)]
    for copy in fills:
        copy.start()
    fold(1)
    tabulate(1)
    analyse(1, 0)
    analyse(1, 1)
    fetches[2 * SLOTS].wait()

    @pl.loop(0, CHUNKS + S_LAG)
    def _(step):
        @pl.when(step + Z_AHEAD < CHUNKS)
        def _():
            stage_z(step + Z_AHEAD)

        for stage_of, lag in ((stage_y, 0), (stage_f, F_LAG), (stage_s, S_LAG)):
            k = step - lag
            valid = jnp.logical_and(k >= 0, k < CHUNKS)
            live = jnp.logical_or(k < PER_SLOT, upper)

            @pl.when(jnp.logical_and(valid, live))
            def _():
                stage_of(k)

    for copy in fills:
        copy.wait()

    @pl.loop(0, CHUNKS)
    def _(k):
        def returned():
            for i in range(2):
                y_first(k, i).wait_send()
                y_second(k, i).wait_send()
            drain(ms.at[k], MA - 1)
            m_own(k).wait()

        @pl.when(k < PER_SLOT)
        def _():
            drain(zs.at[k], MA - 1)
            returned()
            drain(mr.at[k], MA - 1)

        @pl.when(jnp.logical_and(k >= PER_SLOT, upper))
        def _():
            drain(zs.at[k], MA // 2 - 1)
            returned()
            drain(mr.at[k], MA // 2 - 1)

        @pl.when(jnp.logical_and(k >= PER_SLOT, jnp.logical_not(upper)))
        def _():
            drain(zs.at[k], MA // 2)
            drain(mr.at[k], MA // 2)


def per_device(nonlinear, legendre, inverse, orders):
    tile = (ROWS, LANES)
    dma = pltpu.SemaphoreType.DMA
    field = nonlinear.reshape(SLOTS, 2 * THETA * PARTS, LANES)
    values = legendre.reshape(SLOTS, THETA, PARITIES, BLOCKS, LANES).transpose(0, 1, 3, 2, 4)
    values = values.reshape(SLOTS, THETA * BLOCKS * PARITIES, LANES)
    solved = pl.pallas_call(
        kernel,
        out_shape=jax.ShapeDtypeStruct((SLOTS, PARITIES, MA, HALVES) + tile, jnp.bfloat16),
        in_specs=[pl.BlockSpec(memory_space=pltpu.SMEM)] + [pl.BlockSpec(memory_space=pl.ANY)] * 3,
        out_specs=pl.BlockSpec(memory_space=pl.ANY),
        scratch_shapes=[
            pltpu.VMEM((SLOTS, 2) + field.shape[1:], jnp.bfloat16),
            pltpu.VMEM(field.shape[1:], jnp.float32),
            pltpu.VMEM((PARITIES, THETA, PARTS * LANES), jnp.bfloat16),
            pltpu.VMEM((PARITIES, THETA, DEGREES), jnp.bfloat16),
            pltpu.VMEM((DEGREES * PARTS, LANES), jnp.float32),
            pltpu.VMEM((SLOTS, PARITIES, MA, HALVES) + tile, jnp.bfloat16),
            pltpu.VMEM((CHUNKS, YN, MA) + tile, jnp.bfloat16),
            pltpu.VMEM((CHUNKS, MA) + tile, jnp.bfloat16),
            pltpu.VMEM(inverse.shape, jnp.bfloat16),
            pltpu.VMEM((MA // 2,) + tile, jnp.bfloat16),
            dma((CHUNKS,)), dma((CHUNKS,)),
            dma((CHUNKS, 4)), dma((CHUNKS, 4)),
            dma((CHUNKS,)), dma((CHUNKS,)),
            dma((2, CHUNKS)),
            dma((2 * SLOTS + 1,)),
            dma((PER_SLOT,)),
        ],
        compiler_params=pltpu.CompilerParams(collective_id=0, has_side_effects=True, vmem_limit_bytes=52 * 1024 * 1024),
    )(orders, field, values, inverse)
    return solved.reshape(SLOTS, PARITIES, DEGREES, PARTS, LANES)


def solution(mesh):
    in_specs = (
        P("ma", None, None, "row"),
        P("ma", None, None, None),
        P(None, "ma", None, "row", None),
        P("ma"),
    )
    out_specs = P("ma", None, None, None, "row")
    return jax.shard_map(
        per_device, mesh=mesh, in_specs=in_specs, out_specs=out_specs, check_vma=False
    )
```

time: 127 us -> 113 us (0.89)
  Pallas kernels: 123 us -> 109 us
    pallas_call x1, Pallas kernels: 123 us -> 109 us  [per_device(): pl.pallas_call(kernel, out_shape=jax.ShapeDtypeStruct((SLOTS, PARITIES, M...]
where the time goes in v3:
time: 113 us
  Pallas kernels  109 us (96%)
  local copies, waits for them, and re-layouts  4.28 us (4%)
    pallas_call x1, Pallas kernels, per_device(): pl.pallas_call(kernel, out_shape=jax.ShapeDtypeStruct((SLOTS, PARITIES, M...  109 us
    unnamed x3, local copies, waits for them, and re-layouts  4.28 us

profile of v3, /device:TPU:1, one launch (start us, length us, event | category | flops | bytes accessed | tf_op | source)
XLA Modules:
  0.0 113.4 jit_solution(1371904795450963042)
XLA Ops:
  0.0 0.0 copy-start
  0.0 0.7 copy-done
  0.7 109.1 %shard_map.46 = bf16[2,2,64,2,16,128]{5,4,3,2,1,0:T(8,128)(2,1)} custom-call(s32[2]{0:T(128)S(1)} %copy-done, bf16[2,6144,128]{2,1,0:T(8,128)(2,1)} %bitcast.8, bf16[2,6144,128]{2,1,0:T(8,128)(2,1)} %bitcast.9, bf16[2,8,2,128,512]{4,3,2,1,0:T(8,128)(2,1)} %inverse.1), custom_call_target="tpu_custom_call" | custom-call | tf_op jit(solution)/shard_map/pallas_call | solution.py:257
  109.7 3.6 %copy.7 = bf16[2,2,512,4,128]{4,3,2,1,0:T(4,128)(2,1)} copy(bf16[2,2,512,4,128]{4,3,2,1,0:T(4,128)(2,1)} %bitcast.7) | data formatting | bytes 4194304
Async XLA Ops:
  0.0 0.7 copy-start

commit v4 on v3

--- a/solution.py
+++ b/solution.py
@@ -6,7 +6,9 @@
 from jax.sharding import PartitionSpec as P
 
 MESH = pl.DeviceIdType.MESH
-RING = (4, 3, 5, 2, 6, 1, 7)
+NEAR, FAR = (0, 1, 7, 2), (6, 3, 5, 4)
+OFFSETS = NEAR + FAR
+GROUPS, SIDE = 2, 4
 ZN, ON, YN = 8, 8, 4
 MA = ZN * ON
 SLOTS, PARITIES, HALVES, QUAD = 2, 2, 2, 4
@@ -14,6 +16,8 @@
 CHUNKS = SLOTS * PER_SLOT
 ROWS, LANES = 16, 128
 Z_AHEAD, F_LAG, S_LAG = 4, 1, 2
+PIECES = CHUNKS * GROUPS
+LAST = PIECES - GROUPS
 PARTS = 4
 THETA, FOLD = 768, 256
 DEGREES = 512
@@ -36,7 +40,7 @@
         fetches.append(pltpu.make_async_copy(nonlinear.at[slot], raw.at[slot, 0], load.at[2 * slot]))
         fetches.append(pltpu.make_async_copy(legendre.at[slot], raw.at[slot, 1], load.at[2 * slot + 1]))
     fetches.append(pltpu.make_async_copy(inverse, weights, load.at[2 * SLOTS]))
-    for fetch in fetches:
+    for fetch in fetches[:2]:
         fetch.start()
 
     barrier = pltpu.get_barrier_semaphore()
@@ -55,55 +59,38 @@
         inner = k % PER_SLOT
         return k // PER_SLOT, inner // HALVES, inner % HALVES
 
-    def z_out(k, there):
-        slot, p, h = where(k)
-        return remote(coef.at[slot, p, there, h], gathered.at[k, y, me], zs.at[k], zr.at[k], {"ma": there})
+    def z_out(k, q, beside):
+        slot, p, h = where(k)
+        away = (ZN - OFFSETS[q]) % ZN
+        there = lax.rem(z + away, ZN) * ON + beside
+        return remote(coef.at[slot, p, there, h], gathered.at[k, y, q // SIDE, q % SIDE, o], zs.at[k], zr.at[k, q // SIDE], {"ma": there})
 
     def z_own(k):
         slot, p, h = where(k)
-        return pltpu.make_async_copy(coef.at[slot, p, me, h], gathered.at[k, y, me], own.at[0, k])
-
-    def y_first(k, i):
-        return remote(gathered.at[k, y], gathered.at[k, y], ys.at[k, i], yr.at[k, i], y_peer((1, YN - 1)[i]))
-
-    def y_second(k, i):
+        return pltpu.make_async_copy(coef.at[slot, p, me, h], gathered.at[k, y, 0, 0, o], own.at[0, k])
+
+    def y_first(k, g, i):
+        part = gathered.at[k, y, g]
+        return remote(part, part, ys.at[k, g, i], yr.at[k, g, i], y_peer((1, YN - 1)[i]))
+
+    def y_second(k, g, i):
         origin = lax.rem(y + (YN - 1, 1)[i], YN)
-        part = gathered.at[k, origin, pl.ds((0, MA // 2)[i], MA // 2)]
-        return remote(part, part, ys.at[k, 2 + i], yr.at[k, 2 + i], y_peer((1, YN - 1)[i]))
-
-    def m_out(k, there):
-        slot, p, h = where(k)
-        return remote(solved.at[k, there], out.at[slot, p, me, h], ms.at[k], mr.at[k], {"ma": there})
+        part = gathered.at[k, origin, g, pl.ds((0, SIDE // 2)[i], SIDE // 2)]
+        return remote(part, part, ys.at[k, g, 2 + i], yr.at[k, g, 2 + i], y_peer((1, YN - 1)[i]))
+
+    def m_out(k, g, r, beside):
+        slot, p, h = where(k)
+        away = NEAR[r] + g * (FAR[r] - NEAR[r])
+        there = lax.rem(z + away, ZN) * ON + beside
+        return remote(solved.at[k, g, r, beside], out.at[slot, p, me, h], ms.at[k], mr.at[k], {"ma": there})
 
     def m_own(k):
         slot, p, h = where(k)
-        return pltpu.make_async_copy(solved.at[k, me], out.at[slot, p, me, h], own.at[1, k])
+        return pltpu.make_async_copy(solved.at[k, 0, 0, o], out.at[slot, p, me, h], own.at[1, k])
 
     def drain(sem, count):
-        part = solved.at[0, pl.ds(0, count)]
+        part = coef.at[0, 0, pl.ds(0, count), 0]
         pltpu.make_async_copy(part, part, sem).wait()
-
-    def to_all(copy, k):
-        @pl.loop(0, ON)
-        def _(i):
-            beside = lax.rem(o + i, ON)
-            for n in RING:
-                copy(k, lax.rem(z + n, ZN) * ON + beside).start()
-
-            @pl.when(i > 0)
-            def _():
-                copy(k, z * ON + beside).start()
-
-    def to_upper(copy, k):
-        @pl.loop(0, ON)
-        def _(i):
-            beside = lax.rem(o + i, ON)
-            for n in range(ZN // 2):
-                there = (ZN // 2 + lax.rem(z + n, ZN // 2)) * ON + beside
-
-                @pl.when(there != me)
-                def _():
-                    copy(k, there).start()
 
     def fold(slot):
         fetches[2 * slot].wait()
@@ -122,12 +109,13 @@
             folded[0, b * FOLD:(b + 1) * FOLD, :] = (north + south).astype(jnp.bfloat16)
             folded[1, b * FOLD:(b + 1) * FOLD, :] = (north - south).astype(jnp.bfloat16)
 
-    def tabulate(slot):
+    def widen(slot):
         fetches[2 * slot + 1].wait()
         wide[...] = raw[slot, 1].astype(jnp.float32)
-        for p in range(PARITIES):
-            for b in range(BLOCKS):
-                table[p, :, b * LANES:(b + 1) * LANES] = wide[pl.ds(b * PARITIES + p, THETA, stride=BLOCKS * PARITIES), :].astype(jnp.bfloat16)
+
+    def tabulate(p):
+        for b in range(BLOCKS):
+            table[p, :, b * LANES:(b + 1) * LANES] = wide[pl.ds(b * PARITIES + p, THETA, stride=BLOCKS * PARITIES), :].astype(jnp.bfloat16)
 
     def analyse(slot, p):
         product = lax.dot_general(table[p], folded[p], (((0,), (0,)), ((), ())), preferred_element_type=jnp.float32)
@@ -137,59 +125,89 @@
             stage[pl.ds(c, DEGREES, stride=PARTS), :] = product[:, c * LANES:(c + 1) * LANES]
         coef[slot, p] = stage[...].astype(jnp.bfloat16).reshape(MA, HALVES, ROWS, LANES)
 
-    def solve(k):
+    def solve(k, g):
         slot, p, h = where(k)
         row = lax.broadcasted_iota(jnp.int32, (1, ROWS, LANES), 1)
-        flat = gathered[k].reshape(YN, MA * ROWS, LANES)
+        flat = gathered[k, :, g].reshape(YN, SIDE * ON * ROWS, LANES)
         left = jnp.concatenate([flat[n] for n in range(YN)], axis=1)
         total = None
         for jl in range(QUAD):
             right = weights[p, h * QUAD + jl].reshape(2 * LANES, YN * LANES)
             product = lax.dot_general(left, right, (((1,), (1,)), ((), ())), preferred_element_type=jnp.float32)
-            product = product.reshape(MA, ROWS, 2 * LANES)
+            product = product.reshape(SIDE * ON, ROWS, 2 * LANES)
             for f in range(2):
                 piece = product[:, :, f * LANES:(f + 1) * LANES]
                 total = piece if total is None else jnp.where(row // 2 == jl * 2 + f, piece, total)
-        solved[k] = total.astype(jnp.bfloat16).reshape(MA, ROWS, LANES)
+        solved[k, g] = total.astype(jnp.bfloat16).reshape(SIDE, ON, ROWS, LANES)
 
     def stage_z(k):
-        @pl.when(k < PER_SLOT)
-        def _():
-            to_all(z_out, k)
+        for g in range(GROUPS):
+            @pl.loop(0, ON)
+            def _(i):
+                beside = lax.rem(o + i, ON)
+                for r in range(SIDE):
+                    q = g * SIDE + r
+                    lands = lax.rem(z + (ZN - OFFSETS[q]) % ZN, ZN)
+                    go = jnp.logical_or(k < PER_SLOT, lands >= ZN // 2)
+                    if q == 0:
+                        go = jnp.logical_and(go, i > 0)
+
+                    @pl.when(go)
+                    def _():
+                        z_out(k, q, beside).start()
+
+        @pl.when(jnp.logical_or(k < PER_SLOT, upper))
+        def _():
             z_own(k).start()
 
-        @pl.when(k >= PER_SLOT)
-        def _():
-            to_upper(z_out, k)
-
-            @pl.when(upper)
-            def _():
-                z_own(k).start()
-
-    def stage_y(k):
-        z_own(k).wait()
-        drain(zr.at[k], MA - 1)
+    def stage_y(k, g):
+        @pl.when(g == 0)
+        def _():
+            z_own(k).wait()
+            drain(zr.at[k, 0], SIDE * ON - 1)
+
+        @pl.when(g == 1)
+        def _():
+            drain(zr.at[k, 1], SIDE * ON)
+
         for i in range(2):
-            y_first(k, i).start()
-
-    def stage_f(k):
+            y_first(k, g, i).start()
+
+    def stage_f(k, g):
         for i in range(2):
-            y_first(k, i).wait_recv()
-            y_second(k, i).start()
-
-    def stage_s(k):
+            y_first(k, g, i).wait_recv()
+            y_second(k, g, i).start()
+
+    def stage_s(k, g):
         for i in range(2):
-            y_second(k, i).wait_recv()
-        solve(k)
-        to_all(m_out, k)
-        m_own(k).start()
+            y_second(k, g, i).wait_recv()
+        solve(k, g)
+
+        @pl.loop(0, ON)
+        def _(i):
+            beside = lax.rem(o + i, ON)
+            for r in range(SIDE):
+                if r == 0:
+                    @pl.when(g + i > 0)
+                    def _():
+                        m_out(k, g, r, beside).start()
+                else:
+                    m_out(k, g, r, beside).start()
+
+        @pl.when(g == 0)
+        def _():
+            m_own(k).start()
 
     fold(0)
+    widen(0)
+    for fetch in fetches[2:]:
+        fetch.start()
     tabulate(0)
     analyse(0, 0)
     pl.semaphore_wait(barrier, MA - 1 + 2)
     stage_z(0)
     stage_z(1)
+    tabulate(1)
     analyse(0, 1)
     for k in range(2, Z_AHEAD):
         stage_z(k)
@@ -197,26 +215,31 @@
     fills = [pltpu.make_async_copy(zeros, out.at[1, n // HALVES, pl.ds(0, MA // 2), n % HALVES], fill.at[n]) for n in range(PER_SLOT)]
     for copy in fills:
         copy.start()
+    stage_y(0, 0)
     fold(1)
+    widen(1)
+    tabulate(0)
+    analyse(1, 0)
     tabulate(1)
-    analyse(1, 0)
     analyse(1, 1)
     fetches[2 * SLOTS].wait()
 
-    @pl.loop(0, CHUNKS + S_LAG)
+    @pl.loop(0, PIECES + S_LAG)
     def _(step):
-        @pl.when(step + Z_AHEAD < CHUNKS)
-        def _():
-            stage_z(step + Z_AHEAD)
+        @pl.when(jnp.logical_and(lax.rem(step, GROUPS) == 0, step // GROUPS + Z_AHEAD < CHUNKS))
+        def _():
+            stage_z(step // GROUPS + Z_AHEAD)
 
         for stage_of, lag in ((stage_y, 0), (stage_f, F_LAG), (stage_s, S_LAG)):
-            k = step - lag
-            valid = jnp.logical_and(k >= 0, k < CHUNKS)
+            t = step - lag
+            k = t // GROUPS
+            g = lax.rem(t + t // LAST, GROUPS)
+            valid = jnp.logical_and(t >= (1 if stage_of is stage_y else 0), t < PIECES)
             live = jnp.logical_or(k < PER_SLOT, upper)
 
             @pl.when(jnp.logical_and(valid, live))
             def _():
-                stage_of(k)
+                stage_of(k, g)
 
     for copy in fills:
         copy.wait()
@@ -224,9 +247,10 @@
     @pl.loop(0, CHUNKS)
     def _(k):
         def returned():
-            for i in range(2):
-                y_first(k, i).wait_send()
-                y_second(k, i).wait_send()
+            for g in range(GROUPS):
+                for i in range(2):
+                    y_first(k, g, i).wait_send()
+                    y_second(k, g, i).wait_send()
             drain(ms.at[k], MA - 1)
             m_own(k).wait()
 
@@ -266,12 +290,12 @@
             pltpu.VMEM((PARITIES, THETA, DEGREES), jnp.bfloat16),
             pltpu.VMEM((DEGREES * PARTS, LANES), jnp.float32),
             pltpu.VMEM((SLOTS, PARITIES, MA, HALVES) + tile, jnp.bfloat16),
-            pltpu.VMEM((CHUNKS, YN, MA) + tile, jnp.bfloat16),
-            pltpu.VMEM((CHUNKS, MA) + tile, jnp.bfloat16),
+            pltpu.VMEM((CHUNKS, YN, GROUPS, SIDE, ON) + tile, jnp.bfloat16),
+            pltpu.VMEM((CHUNKS, GROUPS, SIDE, ON) + tile, jnp.bfloat16),
             pltpu.VMEM(inverse.shape, jnp.bfloat16),
             pltpu.VMEM((MA // 2,) + tile, jnp.bfloat16),
-            dma((CHUNKS,)), dma((CHUNKS,)),
-            dma((CHUNKS, 4)), dma((CHUNKS, 4)),
+            dma((CHUNKS,)), dma((CHUNKS, GROUPS)),
+            dma((CHUNKS, GROUPS, 4)), dma((CHUNKS, GROUPS, 4)),
             dma((CHUNKS,)), dma((CHUNKS,)),
             dma((2, CHUNKS)),
             dma((2 * SLOTS + 1,)),

time: 113 us -> 108 us (0.956)
  Pallas kernels: 109 us -> 103 us
    pallas_call x1, Pallas kernels: 109 us -> 103 us  [per_device(): pl.pallas_call(kernel, out_shape=jax.ShapeDtypeStruct((SLOTS, PARITIES, M...]
where the time goes in v4:
time: 108 us; the launch traced here: 107 us
  Pallas kernels  103 us (95%)
  local copies, waits for them, and re-layouts  4.28 us (4%)
    pallas_call x1, Pallas kernels, per_device(): pl.pallas_call(kernel, out_shape=jax.ShapeDtypeStruct((SLOTS, PARITIES, M...  103 us
    unnamed x3, local copies, waits for them, and re-layouts  4.28 us

profile of v4, /device:TPU:1, one launch (start us, length us, event | category | flops | bytes accessed | tf_op | source)
XLA Modules:
  0.0 107.5 jit_solution(3875693944959245928)
XLA Ops:
  0.0 0.0 copy-start
  0.0 0.7 copy-done
  0.7 103.2 %shard_map.46 = bf16[2,2,64,2,16,128]{5,4,3,2,1,0:T(8,128)(2,1)} custom-call(s32[2]{0:T(128)S(1)} %copy-done, bf16[2,6144,128]{2,1,0:T(8,128)(2,1)} %bitcast.8, bf16[2,6144,128]{2,1,0:T(8,128)(2,1)} %bitcast.9, bf16[2,8,2,128,512]{4,3,2,1,0:T(8,128)(2,1)} %inverse.1), custom_call_target="tpu_custom_call" | custom-call | tf_op jit(solution)/shard_map/pallas_call | solution.py:281
  103.8 3.6 %copy.7 = bf16[2,2,512,4,128]{4,3,2,1,0:T(4,128)(2,1)} copy(bf16[2,2,512,4,128]{4,3,2,1,0:T(4,128)(2,1)} %bitcast.7) | data formatting | bytes 4194304
Async XLA Ops:
  0.0 0.7 copy-start

commit v5 on v4

--- a/solution.py
+++ b/solution.py
@@ -15,7 +15,7 @@
 PER_SLOT = PARITIES * HALVES
 CHUNKS = SLOTS * PER_SLOT
 ROWS, LANES = 16, 128
-Z_AHEAD, F_LAG, S_LAG = 4, 1, 2
+F_LAG, S_LAG = 1, 2
 PIECES = CHUNKS * GROUPS
 LAST = PIECES - GROUPS
 PARTS = 4
@@ -209,7 +209,7 @@
     stage_z(1)
     tabulate(1)
     analyse(0, 1)
-    for k in range(2, Z_AHEAD):
+    for k in range(2, PER_SLOT):
         stage_z(k)
     zeros[...] = jnp.zeros_like(zeros)
     fills = [pltpu.make_async_copy(zeros, out.at[1, n // HALVES, pl.ds(0, MA // 2), n % HALVES], fill.at[n]) for n in range(PER_SLOT)]
@@ -217,24 +217,28 @@
         copy.start()
     stage_y(0, 0)
     fold(1)
+    stage_y(0, 1)
     widen(1)
     tabulate(0)
+    stage_f(0, 0)
     analyse(1, 0)
+    stage_y(1, 0)
+    stage_z(4)
+    stage_z(5)
+    stage_f(0, 1)
     tabulate(1)
     analyse(1, 1)
+    stage_z(6)
+    stage_z(7)
     fetches[2 * SLOTS].wait()
 
-    @pl.loop(0, PIECES + S_LAG)
+    @pl.loop(S_LAG, PIECES + S_LAG)
     def _(step):
-        @pl.when(jnp.logical_and(lax.rem(step, GROUPS) == 0, step // GROUPS + Z_AHEAD < CHUNKS))
-        def _():
-            stage_z(step // GROUPS + Z_AHEAD)
-
-        for stage_of, lag in ((stage_y, 0), (stage_f, F_LAG), (stage_s, S_LAG)):
+        for stage_of, lag, first in ((stage_y, 0, 3), (stage_f, F_LAG, 2), (stage_s, S_LAG, 0)):
             t = step - lag
             k = t // GROUPS
             g = lax.rem(t + t // LAST, GROUPS)
-            valid = jnp.logical_and(t >= (1 if stage_of is stage_y else 0), t < PIECES)
+            valid = jnp.logical_and(t >= first, t < PIECES)
             live = jnp.logical_or(k < PER_SLOT, upper)
 
             @pl.when(jnp.logical_and(valid, live))
@@ -301,7 +305,7 @@
             dma((2 * SLOTS + 1,)),
             dma((PER_SLOT,)),
         ],
-        compiler_params=pltpu.CompilerParams(collective_id=0, has_side_effects=True, vmem_limit_bytes=52 * 1024 * 1024),
+        compiler_params=pltpu.CompilerParams(collective_id=0, has_side_effects=True, vmem_limit_bytes=50 * 1024 * 1024),
     )(orders, field, values, inverse)
     return solved.reshape(SLOTS, PARITIES, DEGREES, PARTS, LANES)
 

time: 108 us -> 103 us (0.954)
  local copies, waits for them, and re-layouts: 4.28 us -> 1.98 us
  Pallas kernels: 103 us -> 101 us
    unnamed x3, local copies, waits for them, and re-layouts: 4.28 us -> 1.98 us
    pallas_call x1, Pallas kernels: 103 us -> 101 us  [per_device(): pl.pallas_call(kernel, out_shape=jax.ShapeDtypeStruct((SLOTS, PARITIES, M...]
where the time goes in v5:
time: 103 us
  Pallas kernels  101 us (98%)
  local copies, waits for them, and re-layouts  1.98 us (2%)
    pallas_call x1, Pallas kernels, per_device(): pl.pallas_call(kernel, out_shape=jax.ShapeDtypeStruct((SLOTS, PARITIES, M...  101 us

profile of v5, /device:TPU:1, one launch (start us, length us, event | category | flops | bytes accessed | tf_op | source)
XLA Modules:
  0.0 102.9 jit_solution(9824835395323734558)
XLA Ops:
  0.0 0.0 copy-start
  0.0 0.7 copy-done
  0.7 101.0 %shard_map.46 = bf16[2,2,64,2,16,128]{5,4,3,2,1,0:T(8,128)(2,1)S(1)} custom-call(s32[2]{0:T(128)S(1)} %copy-done, bf16[2,6144,128]{2,1,0:T(8,128)(2,1)} %bitcast.8, bf16[2,6144,128]{2,1,0:T(8,128)(2,1)} %bitcast.9, bf16[2,8,2,128,512]{4,3,2,1,0:T(8,128)(2,1)} %inverse.1), custom_call_target="tpu_custom_call" | custom-call | tf_op jit(solution)/shard_map/pallas_call | solution.py:285
  101.6 1.3 %copy.7 = bf16[2,2,512,4,128]{4,3,2,1,0:T(4,128)(2,1)} copy(bf16[2,2,512,4,128]{4,3,2,1,0:T(4,128)(2,1)S(1)} %bitcast.7) | data formatting | bytes 4194304
Async XLA Ops:
  0.0 0.7 copy-start

commit v6 on v5

--- a/solution.py
+++ b/solution.py
@@ -148,9 +148,12 @@
                 for r in range(SIDE):
                     q = g * SIDE + r
                     lands = lax.rem(z + (ZN - OFFSETS[q]) % ZN, ZN)
-                    go = jnp.logical_or(k < PER_SLOT, lands >= ZN // 2)
-                    if q == 0:
-                        go = jnp.logical_and(go, i > 0)
+                    if k < PER_SLOT and q > 0:
+                        z_out(k, q, beside).start()
+                        continue
+                    go = i > 0 if q == 0 else i >= 0
+                    if k >= PER_SLOT:
+                        go = jnp.logical_and(go, lands >= ZN // 2)
 
                     @pl.when(go)
                     def _():

time: 103 us -> 103 us (level)
  no operation moved by 1% of the time
where the time goes in v6:
time: 103 us
  Pallas kernels  101 us (98%)
  local copies, waits for them, and re-layouts  1.98 us (2%)
    pallas_call x1, Pallas kernels, per_device(): pl.pallas_call(kernel, out_shape=jax.ShapeDtypeStruct((SLOTS, PARITIES, M...  101 us

profile of v6, /device:TPU:1, one launch (start us, length us, event | category | flops | bytes accessed | tf_op | source)
XLA Modules:
  0.0 103.0 jit_solution(12573087722973734540)
XLA Ops:
  0.0 0.0 copy-start
  0.0 0.7 copy-done
  0.7 101.0 %shard_map.46 = bf16[2,2,64,2,16,128]{5,4,3,2,1,0:T(8,128)(2,1)S(1)} custom-call(s32[2]{0:T(128)S(1)} %copy-done, bf16[2,6144,128]{2,1,0:T(8,128)(2,1)} %bitcast.8, bf16[2,6144,128]{2,1,0:T(8,128)(2,1)} %bitcast.9, bf16[2,8,2,128,512]{4,3,2,1,0:T(8,128)(2,1)} %inverse.1), custom_call_target="tpu_custom_call" | custom-call | tf_op jit(solution)/shard_map/pallas_call | solution.py:288
  101.6 1.3 %copy.7 = bf16[2,2,512,4,128]{4,3,2,1,0:T(4,128)(2,1)} copy(bf16[2,2,512,4,128]{4,3,2,1,0:T(4,128)(2,1)S(1)} %bitcast.7) | data formatting | bytes 4194304
Async XLA Ops:
  0.0 0.7 copy-start
